TPU v7x, 256 devices: a whole 4x4x8 slice. The times are simulated.
256 devices in a mesh: ctx: 32 (over y, x, core), head: 8 (over z).
Axes of the slice: x: 4, y: 4, z: 8, core: 2. Of those that a mesh axis runs over, the one named last changes fastest.
Arguments:
- queries: bfloat16 [4096, 8192], P('ctx', 'head'), may hold values from -90 to 90
- keys: bfloat16 [4096, 1024], P('ctx', 'head'), may hold values from -4 to 4
- values: bfloat16 [4096, 1024], P('ctx', 'head'), may hold values from -5 to 5
- out_grad: bfloat16 [4096, 8192], P('ctx', 'head'), may hold values from -5 to 5
- block_order: int32 [64], replicated, may hold values from 0 to 63, each once
Outputs:
- grads: bfloat16 [4096, 10240], P(('ctx', 'head'))
All inputs are finite; a program needn't handle non-finite values.
Results may differ from a plain program's by a relative error of at most 0.006.
Values may be sent and summed in bfloat16 or wider, within the bound.
No kernel may reach another device: no remote copies, remote signals or barrier semaphores. Data moves between devices by JAX's collectives and lax.ppermute only.
A program may use at most 64 MiB of HBM per device.

v0:
```python
import jax
import jax.numpy as jnp
from jax import lax
from jax.experimental import pallas as pl
from jax.experimental.pallas import tpu as pltpu
from jax.sharding import Mesh, PartitionSpec as P

HD = 128
QGROUP = 8
BLOCK = 64
TOK = 128
CHIPS = 16
HALF = CHIPS * TOK
OWN_BLOCKS = HALF // BLOCK
UNITS = 4
STEP = 1024
SEEN = OWN_BLOCKS
DIAGONAL = SEEN + UNITS
ROWS = QGROUP * BLOCK
NEG = -1e30
SCALE = HD**-0.5
LOG2E = 1.4426950408889634
BF16 = jnp.bfloat16
F32 = jnp.float32


def mm(a, b):
    return jnp.dot(a, b, preferred_element_type=F32)


def mm_t(a, b):
    return lax.dot_general(a, b, (((1,), (1,)), ((), ())), preferred_element_type=F32)


def fold(x, op):
    return op(x.reshape(x.shape[0] // 8, 8, x.shape[1]), axis=0)


def step_rows(i):
    return pl.ds(pl.multiple_of(i * STEP, STEP), STEP)


def block_rows(i):
    return pl.ds(pl.multiple_of(i * BLOCK, BLOCK), BLOCK)


def prep_kernel(order, place, q_own, q_other, g_own, g_other, meta, rows_qg, owner, upto):
    ctx = place[0]
    core = lax.rem(ctx, 2)

    def clear(p, carry):
        owner[p] = -1
        return carry

    lax.fori_loop(0, 2 * OWN_BLOCKS, clear, 0, unroll=True)
    for i in range(OWN_BLOCKS):
        owner[order[(i // 2) * 4 + core * 2 + i % 2]] = i

    def count(p, seen):
        i = owner[p]
        mine = i >= 0

        @pl.when(mine)
        def _():
            meta[i] = seen

        seen = seen + mine.astype(jnp.int32)
        upto[p] = seen
        return seen

    lax.fori_loop(0, 2 * OWN_BLOCKS, count, 0)
    for u in range(UNITS):
        block = order[(ctx + (u // 2) * (1 - 2 * core)) * 2 + u % 2]
        meta[SEEN + u] = upto[block]
        meta[DIAGONAL + u] = (owner[block] >= 0).astype(jnp.int32)
        q, g = ((q_own, g_own), (q_other, g_other))[u // 2]
        for h in range(QGROUP):
            part = (slice(u % 2 * BLOCK, (u % 2 + 1) * BLOCK), slice(h * HD, (h + 1) * HD))
            rows = slice(h * BLOCK, (h + 1) * BLOCK)
            rows_qg[0, u, rows, :] = q[part]
            rows_qg[1, u, rows, :] = g[part]


def steps_of(meta, u):
    return (meta[SEEN + u] * BLOCK + STEP - 1) // STEP


def stats_kernel(meta, kv, rows_qg, stats, p_all, dp_all, ks, vs):
    for i in range(OWN_BLOCKS):
        rows = slice(i * BLOCK, (i + 1) * BLOCK)
        dst = block_rows(meta[i])
        ks[dst, :] = kv[rows, :HD]
        vs[dst, :] = kv[rows, HD:]

    def unit(u, carry):
        steps = steps_of(meta, u)
        lane = lax.rem(lax.broadcasted_iota(jnp.int32, (1, ROWS), 1), BLOCK)
        limit = (meta[SEEN + u] - 1) * BLOCK + jnp.where(meta[DIAGONAL + u] > 0, lane, BLOCK - 1)

        def top_step(i, top):
            s = mm_t(ks[step_rows(i), :], rows_qg[0, u])
            key = lax.broadcasted_iota(jnp.int32, s.shape, 0)
            s = jnp.where(key <= limit - i * STEP, s, NEG)
            p_all[u, step_rows(i), :] = s
            return jnp.maximum(top, fold(s, jnp.max))

        top = lax.fori_loop(0, steps, top_step, jnp.full((8, ROWS), NEG, F32))
        top = jnp.max(top, axis=0, keepdims=True)

        def sum_step(i, carry):
            total, delta = carry
            rows = step_rows(i)
            dp = mm_t(vs[rows, :], rows_qg[1, u])
            p = jnp.exp2((p_all[u, rows, :] - top) * (SCALE * LOG2E))
            p_all[u, rows, :] = p
            dp_all[u, rows, :] = dp
            return (total + fold(p, jnp.sum), delta + fold(p * dp, jnp.sum))

        zero = jnp.zeros((8, ROWS), F32)
        total, delta = lax.fori_loop(0, steps, sum_step, (zero, zero))
        stats[u, 0:1, :] = top
        stats[u, 1:2, :] = jnp.sum(total, axis=0, keepdims=True)
        stats[u, 2:3, :] = jnp.sum(delta, axis=0, keepdims=True)
        stats[u, 3:8, :] = jnp.zeros((5, ROWS), F32)
        return carry

    lax.fori_loop(0, UNITS, unit, 0)


def merge(stats, came, u):
    other = lax.rem(u + 2, UNITS)
    top, total, delta = (stats[u, k : k + 1, :] for k in range(3))
    top2, total2, delta2 = (came[other, k : k + 1, :] for k in range(3))
    both = jnp.maximum(top, top2)
    w = jnp.exp2((top - both) * (SCALE * LOG2E))
    w2 = jnp.exp2((top2 - both) * (SCALE * LOG2E))
    inv = 1.0 / (total * w + total2 * w2)
    delta = (delta * w + delta2 * w2) * inv
    return w * inv, delta


def grads_kernel(meta, stats, came, p_all, dp_all, rows_qg, dkv, ds_all, dk, dv, held, sems):
    dk[...] = jnp.zeros((HALF, HD), F32)
    dv[...] = jnp.zeros((HALF, HD), F32)

    def leave(slot, u, i):
        return pltpu.make_async_copy(held.at[slot], ds_all.at[u, step_rows(i)], sems.at[slot])

    def unit(u, count):
        w, delta = merge(stats, came, u)

        def grad_step(i, count):
            slot = lax.rem(count, 2)

            @pl.when(count >= 2)
            def _():
                leave(slot, u, i).wait()

            rows = step_rows(i)
            p = p_all[u, rows, :] * w
            ds = (p * (dp_all[u, rows, :] - delta) * SCALE).astype(BF16)
            held[slot] = ds
            dv[rows, :] += mm(p.astype(BF16), rows_qg[1, u])
            dk[rows, :] += mm(ds, rows_qg[0, u])
            leave(slot, u, i).start()
            return count + 1

        return lax.fori_loop(0, steps_of(meta, u), grad_step, count)

    count = lax.fori_loop(0, UNITS, unit, 0)
    for i in range(OWN_BLOCKS):
        rows = slice(i * BLOCK, (i + 1) * BLOCK)
        src = block_rows(meta[i])
        dkv[rows, :HD] = dk[src, :].astype(BF16)
        dkv[rows, HD:] = dv[src, :].astype(BF16)
    for back in range(2):

        @pl.when(count > back)
        def _():
            leave(lax.rem(count + 1 - back, 2), 0, 0).wait()


def queries_kernel(meta, ks, ds_all, dq_own, dq_other, kt, dqt, held, sems):
    def fetch(u, i):
        rows = slice(i * STEP, (i + 1) * STEP)
        return pltpu.make_async_copy(ds_all.at[u, rows], held.at[u, rows], sems.at[u, i])

    steps = [steps_of(meta, u) for u in range(UNITS)]
    for u in range(UNITS):
        for i in range(HALF // STEP):
            pl.when(i < steps[u])(fetch(u, i).start)
    for j in range(HALF // STEP):
        kt[j] = ks[j * STEP : (j + 1) * STEP, :].T
    for u in range(UNITS):
        dqt[...] = jnp.zeros((HD, ROWS), F32)
        for i in range(HALF // STEP):

            @pl.when(i < steps[u])
            def _():
                fetch(u, i).wait()
                dqt[...] += mm(kt[i], held[u, i * STEP : (i + 1) * STEP, :])

        dq = (dq_own, dq_other)[u // 2]
        out = dqt[...].T
        for h in range(QGROUP):
            part = (slice(u % 2 * BLOCK, (u % 2 + 1) * BLOCK), slice(h * HD, (h + 1) * HD))
            dq[part] = out[h * BLOCK : (h + 1) * BLOCK, :]


def call(kernel, ins, outs, scratch, flops, exps, args, limit=10):
    space = {"s": pltpu.SMEM, "v": pltpu.VMEM, "h": pltpu.HBM}
    spec = {k: pl.BlockSpec(memory_space=m) for k, m in space.items()}
    return pl.pallas_call(
        kernel,
        out_shape=tuple(jax.ShapeDtypeStruct(shape, dtype) for _, shape, dtype in outs),
        in_specs=[spec[k] for k in ins],
        out_specs=tuple(spec[k] for k, _, _ in outs),
        scratch_shapes=[
            pltpu.SemaphoreType.DMA(shape) if k == "d" else space[k](shape, dtype) for k, shape, dtype in scratch
        ],
        compiler_params=pltpu.CompilerParams(vmem_limit_bytes=limit * 2**20),
        cost_estimate=pl.CostEstimate(flops=flops, bytes_accessed=2**21, transcendentals=exps),
        name=kernel.__name__,
    )(*args)


def spread_kernel(keys, values, out, k, v, sems):
    copies = [pltpu.make_async_copy(src, dst, sems.at[i]) for i, (src, dst) in enumerate(((keys, k), (values, v)))]
    for copy in copies:
        copy.start()
    for copy in copies:
        copy.wait()
    for i in range(CHIPS):
        out[i, :, :HD] = k[...]
        out[i, :, HD:] = v[...]


def spread(keys, values):
    return pl.pallas_call(
        spread_kernel,
        out_shape=jax.ShapeDtypeStruct((CHIPS, TOK, 2 * HD), BF16),
        in_specs=[pl.BlockSpec(memory_space=pltpu.HBM)] * 2,
        out_specs=pl.BlockSpec(memory_space=pltpu.VMEM),
        scratch_shapes=[pltpu.VMEM((TOK, HD), BF16), pltpu.VMEM((TOK, HD), BF16), pltpu.SemaphoreType.DMA((2,))],
        compiler_params=pltpu.CompilerParams(vmem_limit_bytes=56 * 2**20),
        name="spread_kernel",
    )(keys, values)


def prepare(order, place, q_own, q_other, g_own, g_other):
    row = ("v", (2, UNITS, ROWS, HD), BF16)
    words = ("s", (2 * OWN_BLOCKS,), jnp.int32)
    return call(
        prep_kernel, "ssvvvv", [words, row], [words, words], 0, 0,
        (order, place, q_own, q_other, g_own, g_other),
    )


def key_grads(prepared, kv, swap):
    meta, rows_qg = prepared
    pairs = UNITS * ROWS * HALF
    table = ("v", (UNITS, HALF, ROWS), F32)
    keys = ("v", (HALF, HD), BF16)
    sums = ("v", (HALF, HD), F32)
    stats, p_all, dp_all, ks = call(
        stats_kernel, "svv", [("v", (UNITS, 8, ROWS), F32), table, table, keys], [keys],
        4 * pairs * HD, pairs, (meta, kv, rows_qg),
    )
    came = swap(stats)
    dkv, ds_all = call(
        grads_kernel, "svvvvv", [("v", (HALF, 2 * HD), BF16), ("h", (4 * UNITS, HALF, ROWS), BF16)],
        [sums, sums, ("v", (2, STEP, ROWS), BF16), ("d", (2,), None)],
        4 * pairs * HD, 0, (meta, stats, came, p_all, dp_all, rows_qg),
    )
    return dkv, ks, ds_all


def query_grads(meta, ks, ds_all):
    out = ("v", (TOK, QGROUP * HD), F32)
    scratch = [
        ("v", (HALF // STEP, HD, STEP), BF16),
        ("v", (HD, ROWS), F32),
        ("v", (UNITS, HALF, ROWS), BF16),
        ("d", (UNITS, HALF // STEP), None),
    ]
    return call(
        queries_kernel, "svh", [out, out], scratch, 2 * UNITS * ROWS * HALF * HD, 0, (meta, ks, ds_all), 40
    )


def shards(queries, keys, values, out_grad, block_order):
    plane = ("y", "x")

    def swap(x):
        return lax.ppermute(x, "core", [(0, 1), (1, 0)])

    q_other, g_other = swap(queries), swap(out_grad)
    kv = lax.all_to_all(spread(keys, values), plane, 0, 0, tiled=True).reshape(HALF, 2 * HD)
    place = lax.axis_index(("y", "x", "core")).astype(jnp.int32).reshape(1)
    prepared = prepare(block_order, place, queries, q_other, out_grad, g_other)
    dkv, ks, ds_all = key_grads(prepared, kv, swap)
    parts = lax.all_to_all(dkv.reshape(CHIPS, TOK, 2 * HD), plane, 0, 0, tiled=True)
    dq_own, dq_other = query_grads(prepared[0], ks, ds_all)
    dq = (dq_own + swap(dq_other)).astype(BF16)
    dkv = jnp.sum(parts.astype(F32), axis=0).astype(BF16)
    mine = jnp.concatenate([dq, dkv], axis=1).reshape(8, TOK // 8, 10 * HD)
    got = lax.all_to_all(mine, "head", 0, 0, tiled=True).transpose(1, 0, 2)
    cols = [got[:, :, : 8 * HD], got[:, :, 8 * HD : 9 * HD], got[:, :, 9 * HD :]]
    return jnp.concatenate([c.reshape(TOK // 8, -1) for c in cols], axis=1)


def solution(mesh):
    split = Mesh(mesh.devices.reshape(4, 4, 2, 8), ("y", "x", "core", "head"))
    ctx = ("y", "x", "core")
    rows = P(ctx, "head")
    return jax.shard_map(
        shards,
        mesh=split,
        in_specs=(rows, rows, rows, rows, P()),
        out_specs=P(ctx + ("head",), None),
        check_vma=False,
    )
```

profile of v0, /device:TPU:2, one launch (start us, length us, event | category | flops | bytes accessed | tf_op | source)
XLA Modules:
  0.0 85.6 jit_solution(5254883305255065705)
XLA Ops:
  0.0 1.9 %spread_kernel.1 = bf16[16,128,256]{2,1,0:T(8,128)(2,1)} custom-call(bf16[128,128]{1,0:T(8,128)(2,1)} %keys.1, bf16[128,128]{1,0:T(8,128)(2,1)} %values.1), custom_call_target="tpu_custom_call" | custom-call | tf_op jit(solution)/shard_map/spread_kernel/pallas_call | solution.py:239
  1.9 7.5 %all-to-all-start = ((bf16[16,128,256]{2,1,0:T(8,128)(2,1)}), bf16[16,128,256]{2,1,0:T(8,128)(2,1)S(1)}, u32[]{:S(2)}, u32[]{:S(2)}) async-start(bf16[16,128,256]{2,1,0:T(8,128)(2,1)} %spread_kernel.1), calls=%async_computation | async-start | bytes 2097152 | tf_op jit(solution)/shard_map/all_to_all | solution.py:298
  9.4 0.0 collective-permute-start
  9.4 0.5 collective-permute-start.1
  9.9 1.2 %collective-permute-done.q_other = bf16[128,1024]{1,0:T(8,128)(2,1)S(1)} collective-permute-done((bf16[128,1024]{1,0:T(8,128)(2,1)}, bf16[128,1024]{1,0:T(8,128)(2,1)S(1)}, u32[]{:S(2)}, u32[]{:S(2)}) %collective-permute-start) | collective-permute-done | bytes 262176 | tf_op jit(solution)/shard_map/ppermute | solution.py:295
  11.2 0.4 collective-permute-done.1.g_other
  11.5 0.0 copy-start
  11.5 0.9 %copy-done = bf16[128,1024]{1,0:T(8,128)(2,1)S(1)} copy-done((bf16[128,1024]{1,0:T(8,128)(2,1)S(1)}, bf16[128,1024]{1,0:T(8,128)(2,1)}, u32[]{:S(2)}) %copy-start) | copy-done | bytes 262168
  12.5 0.0 copy-start.1
  12.5 0.9 %copy-done.1 = bf16[128,1024]{1,0:T(8,128)(2,1)S(1)} copy-done((bf16[128,1024]{1,0:T(8,128)(2,1)S(1)}, bf16[128,1024]{1,0:T(8,128)(2,1)}, u32[]{:S(2)}) %copy-start.1) | copy-done | bytes 262168
  13.4 0.0 copy-start.2
  13.4 0.7 copy-done.2
  14.1 1.9 %prep_kernel.1 = (s32[64]{0:T(128)S(1)}, bf16[2,4,512,128]{3,2,1,0:T(8,128)(2,1)S(1)}) custom-call(s32[64]{0:T(128)S(1)} %copy-done.2, s32[1]{0:T(128)} %bitcast.place, bf16[128,1024]{1,0:T(8,128)(2,1)S(1)} %copy-done, bf16[128,1024]{1,0:T(8,128)(2,1)S(1)} %collective-permute-done.q_other, bf16[128,1024]{1,0:T(8,128)(2,1)S(1)} %copy-done.1, ...), custom_call_target="tpu_custom_call" | custom-call | bytes 2097152 | tf_op jit(solution)/shard_map/prep_kernel/pallas_call | solution.py:213
  16.0 9.2 %all-to-all-done = bf16[16,128,256]{2,1,0:T(8,128)(2,1)S(1)} async-done(((bf16[16,128,256]{2,1,0:T(8,128)(2,1)}), bf16[16,128,256]{2,1,0:T(8,128)(2,1)S(1)}, u32[]{:S(2)}, u32[]{:S(2)}) %all-to-all-start) | async-done | bytes 1048608 | tf_op jit(solution)/shard_map/all_to_all | solution.py:298
  25.2 7.6 %stats_kernel.1 = (f32[4,8,512]{2,1,0:T(8,128)S(1)}, f32[4,2048,512]{2,1,0:T(8,128)S(1)}, f32[4,2048,512]{2,1,0:T(8,128)S(1)}, bf16[2048,128]{1,0:T(8,128)(2,1)S(1)}) custom-call(s32[64]{0:T(128)S(1)} %get-tuple-element.15.meta, bf16[2048,256]{1,0:T(8,128)(2,1)S(1)} %bitcast.16, bf16[2,4,512,128]{3,2,1,0:T(8,128)(2,1)S(1)} %get-tuple-element.16.rows_qg), custom_call_target="tpu_custom_call" | custom-call | flops 2147483648 | bytes 2097152 | tf_op jit(solution)/shard_map/stats_kernel/pallas_call | solution.py:213
  32.8 0.1 collective-permute-start.2
  32.9 1.2 %collective-permute-done.2.came = f32[4,8,512]{2,1,0:T(8,128)S(1)} collective-permute-done((f32[4,8,512]{2,1,0:T(8,128)S(1)}, f32[4,8,512]{2,1,0:T(8,128)S(1)}, u32[]{:S(2)}, u32[]{:S(2)}) %collective-permute-start.2) | collective-permute-done | bytes 65568 | tf_op jit(solution)/shard_map/ppermute | solution.py:295
  34.1 8.5 %grads_kernel.1 = (bf16[2048,256]{1,0:T(8,128)(2,1)}, bf16[16,2048,512]{2,1,0:T(8,128)(2,1)}) custom-call(s32[64]{0:T(128)S(1)} %get-tuple-element.15.meta, f32[4,8,512]{2,1,0:T(8,128)S(1)} %get-tuple-element.18.stats, f32[4,8,512]{2,1,0:T(8,128)S(1)} %collective-permute-done.2.came, f32[4,2048,512]{2,1,0:T(8,128)S(1)} %get-tuple-element.19.p_all, ...), custom_call_target="tpu_custom_call" | custom-call | flops 2147483648 | bytes 2097152 | tf_op jit(solution)/shard_map/grads_kernel/pallas_call | solution.py:213
  42.6 5.4 %all-to-all-start.1 = ((bf16[16,128,256]{2,1,0:T(8,128)(2,1)}), bf16[16,128,256]{2,1,0:T(8,128)(2,1)S(1)}, u32[]{:S(2)}, u32[]{:S(2)}) async-start(bf16[16,128,256]{2,1,0:T(8,128)(2,1)} %bitcast.2), calls=%async_computation.1 | async-start | bytes 2097152 | tf_op jit(solution)/shard_map/all_to_all | solution.py:302
  48.0 4.6 %queries_kernel.1 = (f32[128,1024]{1,0:T(8,128)S(1)}, f32[128,1024]{1,0:T(8,128)S(1)}) custom-call(s32[64]{0:T(128)S(1)} %get-tuple-element.15.meta, bf16[2048,128]{1,0:T(8,128)(2,1)S(1)} %get-tuple-element.17.ks, bf16[16,2048,512]{2,1,0:T(8,128)(2,1)} %get-tuple-element.21.ds_all), custom_call_target="tpu_custom_call" | custom-call | flops 1073741824 | bytes 2097152 | tf_op jit(solution)/shard_map/queries_kernel/pallas_call | solution.py:213
  52.6 0.1 collective-permute-start.3
  52.7 1.9 %collective-permute-done.3 = f32[128,1024]{1,0:T(8,128)S(1)} collective-permute-done((f32[128,1024]{1,0:T(8,128)S(1)}, f32[128,1024]{1,0:T(8,128)S(1)}, u32[]{:S(2)}, u32[]{:S(2)}) %collective-permute-start.3) | collective-permute-done | bytes 524320 | tf_op jit(solution)/shard_map/ppermute | solution.py:295
  54.6 0.1 add_convert_fusion
  54.7 9.5 %all-to-all-done.1 = bf16[16,128,256]{2,1,0:T(8,128)(2,1)S(1)} async-done(((bf16[16,128,256]{2,1,0:T(8,128)(2,1)}), bf16[16,128,256]{2,1,0:T(8,128)(2,1)S(1)}, u32[]{:S(2)}, u32[]{:S(2)}) %all-to-all-start.1) | async-done | bytes 1048608 | tf_op jit(solution)/shard_map/all_to_all | solution.py:302
  64.2 0.1 reduce_sum.12
  64.4 20.4 %all_to_all.15 = bf16[8,16,1280]{2,1,0:T(8,128)(2,1)S(1)} all-to-all(bf16[8,16,1280]{2,1,0:T(8,128)(2,1)S(1)} %bitcast.19), channel_id=1, replica_groups=mesh['y'=4,'x'=4,'core'=2,'head'=8] {'head'}, dimensions={0} | all-to-all | bytes 655360 | tf_op jit(solution)/shard_map/all_to_all | solution.py:307
  84.9 0.7 pad_maximum_fusion.1
  (5 shorter events, 0.1 us)
Async XLA Ops:
  1.9 23.3 %all-to-all-start = ((bf16[16,128,256]{2,1,0:T(8,128)(2,1)}), bf16[16,128,256]{2,1,0:T(8,128)(2,1)S(1)}, u32[]{:S(2)}, u32[]{:S(2)}) async-start(bf16[16,128,256]{2,1,0:T(8,128)(2,1)} %spread_kernel.1), calls=%async_computation | async-start | bytes 2097152 | tf_op jit(solution)/shard_map/all_to_all | solution.py:298
  9.4 1.7 %collective-permute-start = (bf16[128,1024]{1,0:T(8,128)(2,1)}, bf16[128,1024]{1,0:T(8,128)(2,1)S(1)}, u32[]{:S(2)}, u32[]{:S(2)}) collective-permute-start(bf16[128,1024]{1,0:T(8,128)(2,1)} %q_own.1), channel_id=1, source_target_pairs={{0,8},{8,0},{1,9},{9,1},{2,10},{10,2},{3,11},{11,3},{4,12},{12,4},... | collective-permute-start | bytes 786440 | tf_op jit(solution)/shard_map/ppermute | solution.py:295
  9.4 2.1 %collective-permute-start.1 = (bf16[128,1024]{1,0:T(8,128)(2,1)}, bf16[128,1024]{1,0:T(8,128)(2,1)S(1)}, u32[]{:S(2)}, u32[]{:S(2)}) collective-permute-start(bf16[128,1024]{1,0:T(8,128)(2,1)} %g_own.1), channel_id=1, source_target_pairs={{0,8},{8,0},{1,9},{9,1},{2,10},{10,2},{3,11},{11,3},{4,12},{12,4},... | collective-permute-start | bytes 786440 | tf_op jit(solution)/shard_map/ppermute | solution.py:295
  11.5 1.0 %copy-start = (bf16[128,1024]{1,0:T(8,128)(2,1)S(1)}, bf16[128,1024]{1,0:T(8,128)(2,1)}, u32[]{:S(2)}) copy-start(bf16[128,1024]{1,0:T(8,128)(2,1)} %q_own.1) | copy-start | bytes 786436
  12.5 0.9 %copy-start.1 = (bf16[128,1024]{1,0:T(8,128)(2,1)S(1)}, bf16[128,1024]{1,0:T(8,128)(2,1)}, u32[]{:S(2)}) copy-start(bf16[128,1024]{1,0:T(8,128)(2,1)} %g_own.1) | copy-start | bytes 786436
  13.4 0.7 copy-start.2
  32.8 1.3 %collective-permute-start.2 = (f32[4,8,512]{2,1,0:T(8,128)S(1)}, f32[4,8,512]{2,1,0:T(8,128)S(1)}, u32[]{:S(2)}, u32[]{:S(2)}) collective-permute-start(f32[4,8,512]{2,1,0:T(8,128)S(1)} %get-tuple-element.18.stats), channel_id=1, source_target_pairs={{0,8},{8,0},{1,9},{9,1},{2,10},{10,2},{3,11},{11,3},{4,12},{12,4},... | collective-permute-start | bytes 196616 | tf_op jit(solution)/shard_map/ppermute | solution.py:295
  42.6 21.6 %all-to-all-start.1 = ((bf16[16,128,256]{2,1,0:T(8,128)(2,1)}), bf16[16,128,256]{2,1,0:T(8,128)(2,1)S(1)}, u32[]{:S(2)}, u32[]{:S(2)}) async-start(bf16[16,128,256]{2,1,0:T(8,128)(2,1)} %bitcast.2), calls=%async_computation.1 | async-start | bytes 2097152 | tf_op jit(solution)/shard_map/all_to_all | solution.py:302
  52.6 2.0 %collective-permute-start.3 = (f32[128,1024]{1,0:T(8,128)S(1)}, f32[128,1024]{1,0:T(8,128)S(1)}, u32[]{:S(2)}, u32[]{:S(2)}) collective-permute-start(f32[128,1024]{1,0:T(8,128)S(1)} %get-tuple-element.23), channel_id=1, source_target_pairs={{0,8},{8,0},{1,9},{9,1},{2,10},{10,2},{3,11},{11,3},{4,12},{12,4},... | collective-permute-start | bytes 1572872 | tf_op jit(solution)/shard_map/ppermute | solution.py:295
where the time goes:
time: 85.7 us; the launch traced here: 85.6 us
  Pallas kernels  24.4 us (28%)
  waiting for transfers between devices  23.5 us (27%)
  blocking collectives  20.4 us (24%)
  starting transfers between devices  13.6 us (16%)
  local copies, waits for them, and re-layouts  2.61 us (3%)
  other arithmetic  0.97 us (1%)
    pallas_call x4, Pallas kernels, call(): pl.pallas_call(kernel, out_shape=tuple((jax.ShapeDtypeStruct(shape, dtype...  22.5 us
    all_to_all x1, blocking collectives, shards(): got = lax.all_to_all(mine, 'head', 0, 0, tiled=True).transpose(1, 0, 2)  20.4 us
    all_to_all x1, waiting for transfers between devices, shards(): lax.all_to_all(dkv.reshape(CHIPS, TOK, 2 * HD), plane, 0, 0, tiled=True)  9.48 us
    all_to_all x1, waiting for transfers between devices, shards(): lax.all_to_all(spread(keys, values), plane, 0, 0, tiled=True)  9.24 us
    all_to_all x1, starting transfers between devices, shards(): lax.all_to_all(spread(keys, values), plane, 0, 0, tiled=True)  7.49 us
    all_to_all x1, starting transfers between devices, shards(): lax.all_to_all(dkv.reshape(CHIPS, TOK, 2 * HD), plane, 0, 0, tiled=True)  5.42 us
    ppermute x4, waiting for transfers between devices, swap(): return lax.ppermute(x, 'core', [(0, 1), (1, 0)])  4.75 us
    unnamed x8, local copies, waits for them, and re-layouts  2.59 us
  transfers between devices with their start and end apart: 6, of which 6 were waited for; matrix products, arithmetic and copies ran while one was open for 0% of the time, Pallas kernels for 8%

commit v1 on v0

--- a/solution.py
+++ b/solution.py
@@ -16,6 +16,7 @@
 STEP = 1024
 SEEN = OWN_BLOCKS
 DIAGONAL = SEEN + UNITS
+PLACE = DIAGONAL + UNITS
 ROWS = QGROUP * BLOCK
 NEG = -1e30
 SCALE = HD**-0.5
@@ -47,6 +48,7 @@
 def prep_kernel(order, place, q_own, q_other, g_own, g_other, meta, rows_qg, owner, upto):
     ctx = place[0]
     core = lax.rem(ctx, 2)
+    meta[PLACE] = ctx
 
     def clear(p, carry):
         owner[p] = -1
@@ -85,12 +87,15 @@
     return (meta[SEEN + u] * BLOCK + STEP - 1) // STEP
 
 
-def stats_kernel(meta, kv, rows_qg, stats, p_all, dp_all, ks, vs):
-    for i in range(OWN_BLOCKS):
-        rows = slice(i * BLOCK, (i + 1) * BLOCK)
-        dst = block_rows(meta[i])
-        ks[dst, :] = kv[rows, :HD]
-        vs[dst, :] = kv[rows, HD:]
+def stats_kernel(meta, k0, k1, k2, k3, v0, v1, v2, v3, rows_qg, stats, p_all, dp_all, ks, vs):
+    y, x = meta[PLACE] // 8, lax.rem(meta[PLACE] // 2, 4)
+    for dy in range(4):
+        for dx in range(4):
+            chip = lax.rem(y + 4 - dy, 4) * 4 + lax.rem(x + 4 - dx, 4)
+            for h in range(2):
+                dst = block_rows(meta[chip * 2 + h])
+                ks[dst, :] = (k0, k1, k2, k3)[dy][dx * TOK + h * BLOCK : dx * TOK + (h + 1) * BLOCK, :]
+                vs[dst, :] = (v0, v1, v2, v3)[dx][dy * TOK + h * BLOCK : dy * TOK + (h + 1) * BLOCK, :]
 
     def unit(u, carry):
         steps = steps_of(meta, u)
@@ -158,7 +163,7 @@
 
             rows = step_rows(i)
             p = p_all[u, rows, :] * w
-            ds = (p * (dp_all[u, rows, :] - delta) * SCALE).astype(BF16)
+            ds = (p * (dp_all[u, rows, :] - delta)).astype(BF16)
             held[slot] = ds
             dv[rows, :] += mm(p.astype(BF16), rows_qg[1, u])
             dk[rows, :] += mm(ds, rows_qg[0, u])
@@ -171,7 +176,7 @@
     for i in range(OWN_BLOCKS):
         rows = slice(i * BLOCK, (i + 1) * BLOCK)
         src = block_rows(meta[i])
-        dkv[rows, :HD] = dk[src, :].astype(BF16)
+        dkv[rows, :HD] = (dk[src, :] * SCALE).astype(BF16)
         dkv[rows, HD:] = dv[src, :].astype(BF16)
     for back in range(2):
 
@@ -201,7 +206,7 @@
                 dqt[...] += mm(kt[i], held[u, i * STEP : (i + 1) * STEP, :])
 
         dq = (dq_own, dq_other)[u // 2]
-        out = dqt[...].T
+        out = dqt[...].T * SCALE
         for h in range(QGROUP):
             part = (slice(u % 2 * BLOCK, (u % 2 + 1) * BLOCK), slice(h * HD, (h + 1) * HD))
             dq[part] = out[h * BLOCK : (h + 1) * BLOCK, :]
@@ -224,27 +229,20 @@
     )(*args)
 
 
-def spread_kernel(keys, values, out, k, v, sems):
-    copies = [pltpu.make_async_copy(src, dst, sems.at[i]) for i, (src, dst) in enumerate(((keys, k), (values, v)))]
-    for copy in copies:
-        copy.start()
-    for copy in copies:
-        copy.wait()
-    for i in range(CHIPS):
-        out[i, :, :HD] = k[...]
-        out[i, :, HD:] = v[...]
-
-
-def spread(keys, values):
-    return pl.pallas_call(
-        spread_kernel,
-        out_shape=jax.ShapeDtypeStruct((CHIPS, TOK, 2 * HD), BF16),
-        in_specs=[pl.BlockSpec(memory_space=pltpu.HBM)] * 2,
-        out_specs=pl.BlockSpec(memory_space=pltpu.VMEM),
-        scratch_shapes=[pltpu.VMEM((TOK, HD), BF16), pltpu.VMEM((TOK, HD), BF16), pltpu.SemaphoreType.DMA((2,))],
-        compiler_params=pltpu.CompilerParams(vmem_limit_bytes=56 * 2**20),
-        name="spread_kernel",
-    )(keys, values)
+def join_kernel(k0, k1, k2, k3, v0, v1, v2, v3, k, v):
+    for out, parts in ((k, (k0, k1, k2, k3)), (v, (v0, v1, v2, v3))):
+        for i, part in enumerate(parts):
+            out[i * TOK : (i + 1) * TOK, :] = part[...]
+
+
+def gather(keys, values):
+    def shifts(v, axis):
+        moved = {s: lax.ppermute(v, axis, [(i, (i + s) % 4) for i in range(4)]) for s in (2, 1, 3)}
+        return (v, moved[1], moved[2], moved[3])
+
+    line = ("v", (4 * TOK, HD), BF16)
+    k, v = call(join_kernel, "v" * 8, [line, line], [], 0, 0, shifts(keys, "x") + shifts(values, "y"))
+    return shifts(k, "y") + shifts(v, "x")
 
 
 def prepare(order, place, q_own, q_other, g_own, g_other):
@@ -263,8 +261,8 @@
     keys = ("v", (HALF, HD), BF16)
     sums = ("v", (HALF, HD), F32)
     stats, p_all, dp_all, ks = call(
-        stats_kernel, "svv", [("v", (UNITS, 8, ROWS), F32), table, table, keys], [keys],
-        4 * pairs * HD, pairs, (meta, kv, rows_qg),
+        stats_kernel, "s" + 9 * "v", [("v", (UNITS, 8, ROWS), F32), table, table, keys], [keys],
+        4 * pairs * HD, pairs, (meta, *kv, rows_qg),
     )
     came = swap(stats)
     dkv, ds_all = call(
@@ -295,7 +293,7 @@
         return lax.ppermute(x, "core", [(0, 1), (1, 0)])
 
     q_other, g_other = swap(queries), swap(out_grad)
-    kv = lax.all_to_all(spread(keys, values), plane, 0, 0, tiled=True).reshape(HALF, 2 * HD)
+    kv = gather(keys, values)
     place = lax.axis_index(("y", "x", "core")).astype(jnp.int32).reshape(1)
     prepared = prepare(block_order, place, queries, q_other, out_grad, g_other)
     dkv, ks, ds_all = key_grads(prepared, kv, swap)

time: 85.7 us -> 96.2 us (1.12); the launches traced: 85.6 us -> 95.1 us
  starting transfers between devices: 13.6 us -> 27.5 us
  waiting for transfers between devices: 23.5 us -> 19.1 us
  Pallas kernels: 24.4 us -> 22.7 us
  local copies, waits for them, and re-layouts: 2.61 us -> 4.13 us
    ppermute x0 -> x12, starting transfers between devices: none -> 19.6 us  [shifts(): lax.ppermute(v, axis, [(i, (i + s) % 4) for i in range(4)])]
    all_to_all x1 -> x0, waiting for transfers between devices: 9.24 us -> none  [shards(): lax.all_to_all(spread(keys, values), plane, 0, 0, tiled=True)]
    all_to_all x1 -> x0, starting transfers between devices: 7.49 us -> none  [shards(): lax.all_to_all(spread(keys, values), plane, 0, 0, tiled=True)]
    ppermute x0 -> x12, waiting for transfers between devices: none -> 6.56 us  [shifts(): lax.ppermute(v, axis, [(i, (i + s) % 4) for i in range(4)])]
    pallas_call x1 -> x0, Pallas kernels: 1.91 us -> none  [spread(): pl.pallas_call(spread_kernel, out_shape=jax.ShapeDtypeStruct((CHIPS, TOK,...]
    all_to_all x1, starting transfers between devices: 5.42 us -> 7.05 us  [shards(): lax.all_to_all(dkv.reshape(CHIPS, TOK, 2 * HD), plane, 0, 0, tiled=True)]
    ppermute x4, waiting for transfers between devices: 4.75 us -> 3.14 us  [swap(): return lax.ppermute(x, 'core', [(0, 1), (1, 0)])]
    unnamed x8 -> x12, local copies, waits for them, and re-layouts: 2.59 us -> 4.1 us
  transfers between devices with their start and end apart: 6 -> 17, of which waited for: 6 -> 6; matrix products, arithmetic and copies ran while one was open for 0% -> 0% of each run, Pallas kernels for 8% -> 7%
where the time goes in v1:
time: 96.2 us; the launch traced here: 95.1 us
  starting transfers between devices  27.5 us (29%)
  Pallas kernels  22.7 us (24%)
  blocking collectives  20.4 us (21%)
  waiting for transfers between devices  19.1 us (20%)
  local copies, waits for them, and re-layouts  4.13 us (4%)
  other arithmetic  0.97 us (1%)
    pallas_call x5, Pallas kernels, call(): pl.pallas_call(kernel, out_shape=tuple((jax.ShapeDtypeStruct(shape, dtype...  22.7 us
    all_to_all x1, blocking collectives, shards(): got = lax.all_to_all(mine, 'head', 0, 0, tiled=True).transpose(1, 0, 2)  20.4 us
    ppermute x12, starting transfers between devices, shifts(): lax.ppermute(v, axis, [(i, (i + s) % 4) for i in range(4)])  19.6 us
    all_to_all x1, waiting for transfers between devices, shards(): lax.all_to_all(dkv.reshape(CHIPS, TOK, 2 * HD), plane, 0, 0, tiled=True)  9.44 us
    all_to_all x1, starting transfers between devices, shards(): lax.all_to_all(dkv.reshape(CHIPS, TOK, 2 * HD), plane, 0, 0, tiled=True)  7.05 us
    ppermute x12, waiting for transfers between devices, shifts(): lax.ppermute(v, axis, [(i, (i + s) % 4) for i in range(4)])  6.56 us
    unnamed x12, local copies, waits for them, and re-layouts  4.1 us
    ppermute x4, waiting for transfers between devices, swap(): return lax.ppermute(x, 'core', [(0, 1), (1, 0)])  3.14 us
  transfers between devices with their start and end apart: 17, of which 6 were waited for; matrix products, arithmetic and copies ran while one was open for 0% of the time, Pallas kernels for 7%

profile of v1, /device:TPU:2, one launch (start us, length us, event | category | flops | bytes accessed | tf_op | source)
XLA Modules:
  0.0 95.1 jit_solution(1771438414569383455)
XLA Ops:
  0.0 0.0 collective-permute-start
  0.0 0.5 collective-permute-start.1
  0.5 2.1 %collective-permute-start.3 = (bf16[128,128]{1,0:T(8,128)(2,1)}, bf16[128,128]{1,0:T(8,128)(2,1)S(1)}, u32[]{:S(2)}, u32[]{:S(2)}) collective-permute-start(bf16[128,128]{1,0:T(8,128)(2,1)} %k0.1), channel_id=1, source_target_pairs={{0,32},{16,48},{32,0},{48,16},{1,33},{17,49},{33,1},{49,17},{2,34}... | collective-permute-start | bytes 98312 | tf_op jit(solution)/shard_map/ppermute | solution.py:240
  2.6 1.6 %collective-permute-start.2 = (bf16[128,128]{1,0:T(8,128)(2,1)}, bf16[128,128]{1,0:T(8,128)(2,1)S(1)}, u32[]{:S(2)}, u32[]{:S(2)}) collective-permute-start(bf16[128,128]{1,0:T(8,128)(2,1)} %k0.1), channel_id=1, source_target_pairs={{0,16},{16,32},{32,48},{48,0},{1,17},{17,33},{33,49},{49,1},{2,18}... | collective-permute-start | bytes 98312 | tf_op jit(solution)/shard_map/ppermute | solution.py:240
  4.2 0.4 collective-permute-start.4
  4.7 1.5 %collective-permute-done.3.k2 = bf16[128,128]{1,0:T(8,128)(2,1)S(1)} collective-permute-done((bf16[128,128]{1,0:T(8,128)(2,1)}, bf16[128,128]{1,0:T(8,128)(2,1)S(1)}, u32[]{:S(2)}, u32[]{:S(2)}) %collective-permute-start.3) | collective-permute-done | bytes 32800 | tf_op jit(solution)/shard_map/ppermute | solution.py:240
  6.1 3.2 %collective-permute-start.6 = (bf16[128,128]{1,0:T(8,128)(2,1)}, bf16[128,128]{1,0:T(8,128)(2,1)S(1)}, u32[]{:S(2)}, u32[]{:S(2)}) collective-permute-start(bf16[128,128]{1,0:T(8,128)(2,1)} %v0.1), channel_id=1, source_target_pairs={{0,128},{64,192},{128,0},{192,64},{1,129},{65,193},{129,1},{193,65... | collective-permute-start | bytes 98312 | tf_op jit(solution)/shard_map/ppermute | solution.py:240
  9.3 0.0 collective-permute-done.2.k1
  9.3 0.7 collective-permute-start.5
  10.0 0.0 collective-permute-done.4.k3
  10.0 2.6 %collective-permute-start.7 = (bf16[128,128]{1,0:T(8,128)(2,1)}, bf16[128,128]{1,0:T(8,128)(2,1)S(1)}, u32[]{:S(2)}, u32[]{:S(2)}) collective-permute-start(bf16[128,128]{1,0:T(8,128)(2,1)} %v0.1), channel_id=1, source_target_pairs={{0,192},{64,0},{128,64},{192,128},{1,193},{65,1},{129,65},{193,129... | collective-permute-start | bytes 98312 | tf_op jit(solution)/shard_map/ppermute | solution.py:240
  12.6 0.0 collective-permute-done.6.v2
  12.6 2.1 %collective-permute-done.5.v1 = bf16[128,128]{1,0:T(8,128)(2,1)S(1)} collective-permute-done((bf16[128,128]{1,0:T(8,128)(2,1)}, bf16[128,128]{1,0:T(8,128)(2,1)S(1)}, u32[]{:S(2)}, u32[]{:S(2)}) %collective-permute-start.5) | collective-permute-done | bytes 32800 | tf_op jit(solution)/shard_map/ppermute | solution.py:240
  14.7 0.0 collective-permute-done.7.v3
  14.7 0.0 copy-start.2
  14.7 0.8 copy-done.2
  15.4 0.0 copy-start.3
  15.4 0.8 copy-done.3
  16.2 3.3 %collective-permute-start.10 = (bf16[512,128]{1,0:T(8,128)(2,1)S(1)}, bf16[512,128]{1,0:T(8,128)(2,1)S(1)}, u32[]{:S(2)}, u32[]{:S(2)}) collective-permute-start(bf16[512,128]{1,0:T(8,128)(2,1)S(1)} %get-tuple-element.18.k0), channel_id=1, source_target_pairs={{0,192},{64,0},{128,64},{192,128},{1,193},{65,1},{129,65},{193,129... | collective-permute-start | bytes 393224 | tf_op jit(solution)/shard_map/ppermute | solution.py:240
  19.5 0.0 collective-permute-start.9
  19.5 1.0 %collective-permute-start.8 = (bf16[512,128]{1,0:T(8,128)(2,1)S(1)}, bf16[512,128]{1,0:T(8,128)(2,1)S(1)}, u32[]{:S(2)}, u32[]{:S(2)}) collective-permute-start(bf16[512,128]{1,0:T(8,128)(2,1)S(1)} %get-tuple-element.18.k0), channel_id=1, source_target_pairs={{0,64},{64,128},{128,192},{192,0},{1,65},{65,129},{129,193},{193,1... | collective-permute-start | bytes 393224 | tf_op jit(solution)/shard_map/ppermute | solution.py:240
  20.5 3.0 %collective-permute-done.10.k3 = bf16[512,128]{1,0:T(8,128)(2,1)S(1)} collective-permute-done((bf16[512,128]{1,0:T(8,128)(2,1)S(1)}, bf16[512,128]{1,0:T(8,128)(2,1)S(1)}, u32[]{:S(2)}, u32[]{:S(2)}) %collective-permute-start.10) | collective-permute-done | bytes 131104 | tf_op jit(solution)/shard_map/ppermute | solution.py:240
  23.5 1.2 %collective-permute-start.13 = (bf16[512,128]{1,0:T(8,128)(2,1)S(1)}, bf16[512,128]{1,0:T(8,128)(2,1)S(1)}, u32[]{:S(2)}, u32[]{:S(2)}) collective-permute-start(bf16[512,128]{1,0:T(8,128)(2,1)S(1)} %get-tuple-element.19.v0), channel_id=1, source_target_pairs={{0,48},{16,0},{32,16},{48,32},{1,49},{17,1},{33,17},{49,33},{2,50}... | collective-permute-start | bytes 393224 | tf_op jit(solution)/shard_map/ppermute | solution.py:240
  24.6 0.0 collective-permute-done.q_other
  24.6 1.8 %collective-permute-start.12 = (bf16[512,128]{1,0:T(8,128)(2,1)S(1)}, bf16[512,128]{1,0:T(8,128)(2,1)S(1)}, u32[]{:S(2)}, u32[]{:S(2)}) collective-permute-start(bf16[512,128]{1,0:T(8,128)(2,1)S(1)} %get-tuple-element.19.v0), channel_id=1, source_target_pairs={{0,32},{16,48},{32,0},{48,16},{1,33},{17,49},{33,1},{49,17},{2,34}... | collective-permute-start | bytes 393224 | tf_op jit(solution)/shard_map/ppermute | solution.py:240
  26.4 0.0 collective-permute-done.1.g_other
  26.4 1.8 %collective-permute-start.11 = (bf16[512,128]{1,0:T(8,128)(2,1)S(1)}, bf16[512,128]{1,0:T(8,128)(2,1)S(1)}, u32[]{:S(2)}, u32[]{:S(2)}) collective-permute-start(bf16[512,128]{1,0:T(8,128)(2,1)S(1)} %get-tuple-element.19.v0), channel_id=1, source_target_pairs={{0,16},{16,32},{32,48},{48,0},{1,17},{17,33},{33,49},{49,1},{2,18}... | collective-permute-start | bytes 393224 | tf_op jit(solution)/shard_map/ppermute | solution.py:240
  28.2 0.0 copy-start
  28.2 0.9 copy-done
  29.2 0.0 copy-start.1
  29.2 0.9 copy-done.1
  30.1 0.0 copy-start.4
  30.1 0.7 copy-done.4
  30.8 1.9 %prep_kernel.1 = (s32[64]{0:T(128)S(1)}, bf16[2,4,512,128]{3,2,1,0:T(8,128)(2,1)S(1)}) custom-call(s32[64]{0:T(128)S(1)} %copy-done.4, s32[1]{0:T(128)} %bitcast.place, bf16[128,1024]{1,0:T(8,128)(2,1)S(1)} %copy-done, bf16[128,1024]{1,0:T(8,128)(2,1)S(1)} %collective-permute-done.q_other, bf16[128,1024]{1,0:T(8,128)(2,1)S(1)} %copy-done.1, ...), custom_call_target="tpu_custom_call" | custom-call | bytes 2097152 | tf_op jit(solution)/shard_map/prep_kernel/pallas_call | solution.py:218
  32.6 0.0 collective-permute-done.9.k2
  32.7 0.0 collective-permute-done.8.k1
  32.7 0.0 collective-permute-done.13.v3
  32.7 0.0 collective-permute-done.12.v2
  32.7 0.0 collective-permute-done.11.v1
  32.7 7.5 %stats_kernel.1 = (f32[4,8,512]{2,1,0:T(8,128)S(1)}, f32[4,2048,512]{2,1,0:T(8,128)S(1)}, f32[4,2048,512]{2,1,0:T(8,128)S(1)}, bf16[2048,128]{1,0:T(8,128)(2,1)S(1)}) custom-call(s32[64]{0:T(128)S(1)} %get-tuple-element.17.meta, bf16[512,128]{1,0:T(8,128)(2,1)S(1)} %get-tuple-element.18.k0, bf16[512,128]{1,0:T(8,128)(2,1)S(1)} %collective-permute-done.8.k1, ...), custom_call_target="tpu_custom_call" | custom-call | flops 2147483648 | bytes 2097152 | tf_op jit(solution)/shard_map/stats_kernel/pallas_call | solution.py:218
  40.2 0.3 collective-permute-start.14
  40.5 1.2 %collective-permute-done.14.came = f32[4,8,512]{2,1,0:T(8,128)S(1)} collective-permute-done((f32[4,8,512]{2,1,0:T(8,128)S(1)}, f32[4,8,512]{2,1,0:T(8,128)S(1)}, u32[]{:S(2)}, u32[]{:S(2)}) %collective-permute-start.14) | collective-permute-done | bytes 65568 | tf_op jit(solution)/shard_map/ppermute | solution.py:293
  41.8 8.7 %grads_kernel.1 = (bf16[2048,256]{1,0:T(8,128)(2,1)}, bf16[16,2048,512]{2,1,0:T(8,128)(2,1)}) custom-call(s32[64]{0:T(128)S(1)} %get-tuple-element.17.meta, f32[4,8,512]{2,1,0:T(8,128)S(1)} %get-tuple-element.22.stats, f32[4,8,512]{2,1,0:T(8,128)S(1)} %collective-permute-done.14.came, f32[4,2048,512]{2,1,0:T(8,128)S(1)} %get-tuple-element.23.p_all, ...), custom_call_target="tpu_custom_call" | custom-call | flops 2147483648 | bytes 2097152 | tf_op jit(solution)/shard_map/grads_kernel/pallas_call | solution.py:218
  50.5 7.1 %all-to-all-start = ((bf16[16,128,256]{2,1,0:T(8,128)(2,1)}), bf16[16,128,256]{2,1,0:T(8,128)(2,1)S(1)}, u32[]{:S(2)}, u32[]{:S(2)}) async-start(bf16[16,128,256]{2,1,0:T(8,128)(2,1)} %bitcast.1), calls=%async_computation | async-start | bytes 2097152 | tf_op jit(solution)/shard_map/all_to_all | solution.py:300
  57.6 4.6 %queries_kernel.1 = (f32[128,1024]{1,0:T(8,128)S(1)}, f32[128,1024]{1,0:T(8,128)S(1)}) custom-call(s32[64]{0:T(128)S(1)} %get-tuple-element.17.meta, bf16[2048,128]{1,0:T(8,128)(2,1)S(1)} %get-tuple-element.21.ks, bf16[16,2048,512]{2,1,0:T(8,128)(2,1)} %get-tuple-element.25.ds_all), custom_call_target="tpu_custom_call" | custom-call | flops 1073741824 | bytes 2097152 | tf_op jit(solution)/shard_map/queries_kernel/pallas_call | solution.py:218
  62.2 0.1 collective-permute-start.15
  62.3 1.9 %collective-permute-done.15 = f32[128,1024]{1,0:T(8,128)S(1)} collective-permute-done((f32[128,1024]{1,0:T(8,128)S(1)}, f32[128,1024]{1,0:T(8,128)S(1)}, u32[]{:S(2)}, u32[]{:S(2)}) %collective-permute-start.15) | collective-permute-done | bytes 524320 | tf_op jit(solution)/shard_map/ppermute | solution.py:293
  64.2 0.1 add_convert_fusion
  64.2 9.4 %all-to-all-done = bf16[16,128,256]{2,1,0:T(8,128)(2,1)S(1)} async-done(((bf16[16,128,256]{2,1,0:T(8,128)(2,1)}), bf16[16,128,256]{2,1,0:T(8,128)(2,1)S(1)}, u32[]{:S(2)}, u32[]{:S(2)}) %all-to-all-start) | async-done | bytes 1048608 | tf_op jit(solution)/shard_map/all_to_all | solution.py:300
  73.7 0.1 reduce_sum.12
  73.8 20.4 %all_to_all.10 = bf16[8,16,1280]{2,1,0:T(8,128)(2,1)S(1)} all-to-all(bf16[8,16,1280]{2,1,0:T(8,128)(2,1)S(1)} %bitcast.17), channel_id=1, replica_groups=mesh['y'=4,'x'=4,'core'=2,'head'=8] {'head'}, dimensions={0} | all-to-all | bytes 655360 | tf_op jit(solution)/shard_map/all_to_all | solution.py:305
  94.4 0.7 pad_maximum_fusion.1
  (6 shorter events, 0.1 us)
Async XLA Ops:
  0.0 24.6 %collective-permute-start = (bf16[128,1024]{1,0:T(8,128)(2,1)}, bf16[128,1024]{1,0:T(8,128)(2,1)S(1)}, u32[]{:S(2)}, u32[]{:S(2)}) collective-permute-start(bf16[128,1024]{1,0:T(8,128)(2,1)} %q_own.1), channel_id=1, source_target_pairs={{0,8},{8,0},{1,9},{9,1},{2,10},{10,2},{3,11},{11,3},{4,12},{12,4},... | collective-permute-start | bytes 786440 | tf_op jit(solution)/shard_map/ppermute | solution.py:293
  0.0 26.4 %collective-permute-start.1 = (bf16[128,1024]{1,0:T(8,128)(2,1)}, bf16[128,1024]{1,0:T(8,128)(2,1)S(1)}, u32[]{:S(2)}, u32[]{:S(2)}) collective-permute-start(bf16[128,1024]{1,0:T(8,128)(2,1)} %g_own.1), channel_id=1, source_target_pairs={{0,8},{8,0},{1,9},{9,1},{2,10},{10,2},{3,11},{11,3},{4,12},{12,4},... | collective-permute-start | bytes 786440 | tf_op jit(solution)/shard_map/ppermute | solution.py:293
  0.5 5.6 %collective-permute-start.3 = (bf16[128,128]{1,0:T(8,128)(2,1)}, bf16[128,128]{1,0:T(8,128)(2,1)S(1)}, u32[]{:S(2)}, u32[]{:S(2)}) collective-permute-start(bf16[128,128]{1,0:T(8,128)(2,1)} %k0.1), channel_id=1, source_target_pairs={{0,32},{16,48},{32,0},{48,16},{1,33},{17,49},{33,1},{49,17},{2,34}... | collective-permute-start | bytes 98312 | tf_op jit(solution)/shard_map/ppermute | solution.py:240
  2.6 6.7 %collective-permute-start.2 = (bf16[128,128]{1,0:T(8,128)(2,1)}, bf16[128,128]{1,0:T(8,128)(2,1)S(1)}, u32[]{:S(2)}, u32[]{:S(2)}) collective-permute-start(bf16[128,128]{1,0:T(8,128)(2,1)} %k0.1), channel_id=1, source_target_pairs={{0,16},{16,32},{32,48},{48,0},{1,17},{17,33},{33,49},{49,1},{2,18}... | collective-permute-start | bytes 98312 | tf_op jit(solution)/shard_map/ppermute | solution.py:240
  4.2 5.8 %collective-permute-start.4 = (bf16[128,128]{1,0:T(8,128)(2,1)}, bf16[128,128]{1,0:T(8,128)(2,1)S(1)}, u32[]{:S(2)}, u32[]{:S(2)}) collective-permute-start(bf16[128,128]{1,0:T(8,128)(2,1)} %k0.1), channel_id=1, source_target_pairs={{0,48},{16,0},{32,16},{48,32},{1,49},{17,1},{33,17},{49,33},{2,50}... | collective-permute-start | bytes 98312 | tf_op jit(solution)/shard_map/ppermute | solution.py:240
  6.1 6.4 %collective-permute-start.6 = (bf16[128,128]{1,0:T(8,128)(2,1)}, bf16[128,128]{1,0:T(8,128)(2,1)S(1)}, u32[]{:S(2)}, u32[]{:S(2)}) collective-permute-start(bf16[128,128]{1,0:T(8,128)(2,1)} %v0.1), channel_id=1, source_target_pairs={{0,128},{64,192},{128,0},{192,64},{1,129},{65,193},{129,1},{193,65... | collective-permute-start | bytes 98312 | tf_op jit(solution)/shard_map/ppermute | solution.py:240
  9.3 5.3 %collective-permute-start.5 = (bf16[128,128]{1,0:T(8,128)(2,1)}, bf16[128,128]{1,0:T(8,128)(2,1)S(1)}, u32[]{:S(2)}, u32[]{:S(2)}) collective-permute-start(bf16[128,128]{1,0:T(8,128)(2,1)} %v0.1), channel_id=1, source_target_pairs={{0,64},{64,128},{128,192},{192,0},{1,65},{65,129},{129,193},{193,1... | collective-permute-start | bytes 98312 | tf_op jit(solution)/shard_map/ppermute | solution.py:240
  10.0 4.7 %collective-permute-start.7 = (bf16[128,128]{1,0:T(8,128)(2,1)}, bf16[128,128]{1,0:T(8,128)(2,1)S(1)}, u32[]{:S(2)}, u32[]{:S(2)}) collective-permute-start(bf16[128,128]{1,0:T(8,128)(2,1)} %v0.1), channel_id=1, source_target_pairs={{0,192},{64,0},{128,64},{192,128},{1,193},{65,1},{129,65},{193,129... | collective-permute-start | bytes 98312 | tf_op jit(solution)/shard_map/ppermute | solution.py:240
  14.7 0.8 copy-start.2
  15.4 0.8 copy-start.3
  16.2 7.2 %collective-permute-start.10 = (bf16[512,128]{1,0:T(8,128)(2,1)S(1)}, bf16[512,128]{1,0:T(8,128)(2,1)S(1)}, u32[]{:S(2)}, u32[]{:S(2)}) collective-permute-start(bf16[512,128]{1,0:T(8,128)(2,1)S(1)} %get-tuple-element.18.k0), channel_id=1, source_target_pairs={{0,192},{64,0},{128,64},{192,128},{1,193},{65,1},{129,65},{193,129... | collective-permute-start | bytes 393224 | tf_op jit(solution)/shard_map/ppermute | solution.py:240
  19.5 13.1 %collective-permute-start.9 = (bf16[512,128]{1,0:T(8,128)(2,1)S(1)}, bf16[512,128]{1,0:T(8,128)(2,1)S(1)}, u32[]{:S(2)}, u32[]{:S(2)}) collective-permute-start(bf16[512,128]{1,0:T(8,128)(2,1)S(1)} %get-tuple-element.18.k0), channel_id=1, source_target_pairs={{0,128},{64,192},{128,0},{192,64},{1,129},{65,193},{129,1},{193,65... | collective-permute-start | bytes 393224 | tf_op jit(solution)/shard_map/ppermute | solution.py:240
  19.5 13.1 %collective-permute-start.8 = (bf16[512,128]{1,0:T(8,128)(2,1)S(1)}, bf16[512,128]{1,0:T(8,128)(2,1)S(1)}, u32[]{:S(2)}, u32[]{:S(2)}) collective-permute-start(bf16[512,128]{1,0:T(8,128)(2,1)S(1)} %get-tuple-element.18.k0), channel_id=1, source_target_pairs={{0,64},{64,128},{128,192},{192,0},{1,65},{65,129},{129,193},{193,1... | collective-permute-start | bytes 393224 | tf_op jit(solution)/shard_map/ppermute | solution.py:240
  23.5 9.2 %collective-permute-start.13 = (bf16[512,128]{1,0:T(8,128)(2,1)S(1)}, bf16[512,128]{1,0:T(8,128)(2,1)S(1)}, u32[]{:S(2)}, u32[]{:S(2)}) collective-permute-start(bf16[512,128]{1,0:T(8,128)(2,1)S(1)} %get-tuple-element.19.v0), channel_id=1, source_target_pairs={{0,48},{16,0},{32,16},{48,32},{1,49},{17,1},{33,17},{49,33},{2,50}... | collective-permute-start | bytes 393224 | tf_op jit(solution)/shard_map/ppermute | solution.py:240
  24.6 8.1 %collective-permute-start.12 = (bf16[512,128]{1,0:T(8,128)(2,1)S(1)}, bf16[512,128]{1,0:T(8,128)(2,1)S(1)}, u32[]{:S(2)}, u32[]{:S(2)}) collective-permute-start(bf16[512,128]{1,0:T(8,128)(2,1)S(1)} %get-tuple-element.19.v0), channel_id=1, source_target_pairs={{0,32},{16,48},{32,0},{48,16},{1,33},{17,49},{33,1},{49,17},{2,34}... | collective-permute-start | bytes 393224 | tf_op jit(solution)/shard_map/ppermute | solution.py:240
  26.4 6.3 %collective-permute-start.11 = (bf16[512,128]{1,0:T(8,128)(2,1)S(1)}, bf16[512,128]{1,0:T(8,128)(2,1)S(1)}, u32[]{:S(2)}, u32[]{:S(2)}) collective-permute-start(bf16[512,128]{1,0:T(8,128)(2,1)S(1)} %get-tuple-element.19.v0), channel_id=1, source_target_pairs={{0,16},{16,32},{32,48},{48,0},{1,17},{17,33},{33,49},{49,1},{2,18}... | collective-permute-start | bytes 393224 | tf_op jit(solution)/shard_map/ppermute | solution.py:240
  28.2 0.9 copy-start
  29.2 0.9 copy-start.1
  30.1 0.7 copy-start.4
  40.2 1.5 %collective-permute-start.14 = (f32[4,8,512]{2,1,0:T(8,128)S(1)}, f32[4,8,512]{2,1,0:T(8,128)S(1)}, u32[]{:S(2)}, u32[]{:S(2)}) collective-permute-start(f32[4,8,512]{2,1,0:T(8,128)S(1)} %get-tuple-element.22.stats), channel_id=1, source_target_pairs={{0,8},{8,0},{1,9},{9,1},{2,10},{10,2},{3,11},{11,3},{4,12},{12,4},... | collective-permute-start | bytes 196616 | tf_op jit(solution)/shard_map/ppermute | solution.py:293
  50.5 23.2 %all-to-all-start = ((bf16[16,128,256]{2,1,0:T(8,128)(2,1)}), bf16[16,128,256]{2,1,0:T(8,128)(2,1)S(1)}, u32[]{:S(2)}, u32[]{:S(2)}) async-start(bf16[16,128,256]{2,1,0:T(8,128)(2,1)} %bitcast.1), calls=%async_computation | async-start | bytes 2097152 | tf_op jit(solution)/shard_map/all_to_all | solution.py:300
  62.2 2.0 %collective-permute-start.15 = (f32[128,1024]{1,0:T(8,128)S(1)}, f32[128,1024]{1,0:T(8,128)S(1)}, u32[]{:S(2)}, u32[]{:S(2)}) collective-permute-start(f32[128,1024]{1,0:T(8,128)S(1)} %get-tuple-element.27), channel_id=1, source_target_pairs={{0,8},{8,0},{1,9},{9,1},{2,10},{10,2},{3,11},{11,3},{4,12},{12,4},... | collective-permute-start | bytes 1572872 | tf_op jit(solution)/shard_map/ppermute | solution.py:293
